TPU v7x, 128 devices: a whole 4x4x4 slice. The times are simulated.
128 devices in a mesh: item: 32 (over z, x, core), dim: 4 (over y).
Axes of the slice: x: 4, y: 4, z: 4, core: 2. Of those that a mesh axis runs over, the one named last changes fastest.
Arguments:
- embeddings: float32 [131072, 512], P('item', 'dim'), as said below
- cand_index: int32 [3, 1024], P(None, 'item'), may hold values from 0 to 4095
- cand_count: int32 [3, 32], replicated, may hold values from 1 to 32, 512 in all within a row
Outputs:
- weights: float32 [3, 131072], P(None, ('item', 'dim'))
Inputs may be any that keep to these rules, and one draw needn't show every extreme that they name: `cand_index`: row numbers within one index of item's own 4096 rows; unused slots also hold such numbers. `cand_count`: in every round the counts add up to 512 and the largest is exactly 32. `embeddings`: finite values.
All inputs are finite; a program needn't handle non-finite values.
Results may differ from a plain program's by a relative error of at most 0.00018.
Values sent between devices are 32-bit elements; how exact they have to be, the bound alone decides.
A program may use at most 192 MiB of HBM per device.

v0:
```python
import itertools

import jax
import jax.numpy as jnp
from jax import lax
from jax.experimental import pallas as pl
from jax.experimental.pallas import tpu as pltpu
from jax.sharding import PartitionSpec as P

CAP = 4.0
MESH = pl.DeviceIdType.MESH
ROUNDS = 3
SLOTS = 32
LANES = 128
ITEMS = 32
ROWS = 4096
SHARE = 1024
STEP = 256
PIECES = SHARE // STEP
TOTAL = 131072
TILE = 8
TILES_SLOTS = SLOTS // TILE
BLOCK = 4 * TILES_SLOTS
TILES = 92
USED = TILES * 8
GROUP = 4
BF16 = jnp.bfloat16
F32 = jnp.float32


def kernel(
    index_hbm, count_hbm, x_ref, out_ref,
    index_ref, count_ref, ordered, table, xv, xfull, relay_buf, cand_0, cand_1, cand_2,
    ch, cl, nrm, xh, xl, sq, low, done, part, red_line, red_plane,
    load_sem, send_sem, recv_sem,
):
    cand = (cand_0, cand_1, cand_2)
    item, dim = lax.axis_index("item"), lax.axis_index("dim")
    z, x, core = item // 8, (item // 2) % 4, item % 2
    a = x * (1 - core) + z * core
    b = z * (1 - core) + x * core

    def device(a_, b_):
        return (a_ * (2 + 6 * core) + b_ * (8 - 6 * core) + core, dim)

    def block(b_, a_):
        return ((core * 4 + b_) * 4 + a_) * BLOCK

    a_up, a_down = (a + 1) % 4, (a + 3) % 4
    b_up, b_down, b_far = (b + 1) % 4, (b + 3) % 4, (b + 2) % 4
    y_up, y_down, y_far = (dim + 1) % 4, (dim + 3) % 4, (dim + 2) % 4
    sibling = (item + 1 - 2 * core, dim)
    rank_line, rank_plane = dim * 2 + core, item // 2

    def line_device(step):
        other = (rank_line + step) % 8
        return (item - core + other % 2, other // 2)

    def plane_device(step):
        return (((rank_plane + step) % 16) * 2 + core, dim)

    loads = [
        pltpu.make_async_copy(index_hbm, index_ref, load_sem.at[0]),
        pltpu.make_async_copy(x_ref, xv, load_sem.at[1]),
        pltpu.make_async_copy(count_hbm, count_ref, load_sem.at[2]),
        pltpu.make_async_copy(x_ref.at[pl.ds(dim * SHARE, SHARE)], xfull.at[dim], load_sem.at[3]),
    ]
    for copy in loads:
        copy.start()
    index_load, x_load, count_load, own_rows = loads

    barrier = pltpu.get_barrier_semaphore()
    for step in range(1, 8):
        pl.semaphore_signal(barrier, inc=1, device_id=line_device(step), device_id_type=MESH)
    for step in range(1, 16):
        pl.semaphore_signal(barrier, inc=1, device_id=plane_device(step), device_id_type=MESH)

    index_load.wait()
    x_load.wait()
    for r in range(ROUNDS):
        def pick(g, carry, r=r):
            rows = [xv[pl.ds(index_ref[r, g * TILE + k], 1), :] for k in range(TILE)]
            cand[r][block(b, a) + dim * TILES_SLOTS + g] = jnp.concatenate(rows, axis=0)
            return carry

        lax.fori_loop(0, TILES_SLOTS, pick, 0)
    pl.semaphore_wait(barrier, 22)

    number = itertools.count()
    started = []

    def send(src, dst, target):
        k = next(number)
        copy = pltpu.make_async_remote_copy(
            src_ref=src, dst_ref=dst, send_sem=send_sem.at[k], recv_sem=recv_sem.at[k],
            device_id=target, device_id_type=MESH,
        )
        copy.start()
        started.append(copy)
        return copy

    def send_cand(r, start, length, target):
        ref = cand[r].at[pl.ds(start, length)]
        return send(ref, ref, target)

    y_copies, first, second_up, second_down, pass_up, pass_down, swap = [{} for _ in range(7)]
    relay, near, passed = [{} for _ in range(3)]

    def pick_send(r):
        start = block(b, a) + dim * TILES_SLOTS
        y_copies[r] = [send_cand(r, start, TILES_SLOTS, (item, (dim + d) % 4)) for d in (1, 3, 2)]

    half = STEP // 2

    def near_send(t):
        lands = xfull.at[dim, pl.ds(t * STEP, STEP)]
        near[t] = (
            send(xv.at[pl.ds(y_up * SHARE + t * STEP, STEP)], lands, (item, y_up)),
            send(xv.at[pl.ds(y_down * SHARE + t * STEP, STEP)], lands, (item, y_down)),
        )

    def far_send(t):
        far = y_far * SHARE + t * STEP
        relay[t] = (
            send(xv.at[pl.ds(far, half)], relay_buf.at[0, t], (item, y_up)),
            send(xv.at[pl.ds(far + half, half)], relay_buf.at[1, t], (item, y_down)),
        )

    def far_pass(t):
        relay[t][0].wait_recv()
        up = send(relay_buf.at[0, t], xfull.at[y_down, pl.ds(t * STEP, half)], (item, y_up))
        relay[t][1].wait_recv()
        down = send(relay_buf.at[1, t], xfull.at[y_up, pl.ds(t * STEP + half, half)], (item, y_down))
        passed[t] = (up, down)

    def first_send(r):
        for copy in y_copies[r]:
            copy.wait_recv()
        first[r] = [send_cand(r, block(b, a), BLOCK, device(a_, b)) for a_ in (a_up, a_down)]

    def first_pass(r):
        first[r][0].wait_recv()
        up = send_cand(r, block(b, a_down), BLOCK // 2, device(a_up, b))
        first[r][1].wait_recv()
        down = send_cand(r, block(b, a_up) + BLOCK // 2, BLOCK // 2, device(a_down, b))
        first[r] = (up, down)

    def second_send(r):
        for copy in first[r]:
            copy.wait_recv()
        second_up[r] = send_cand(r, block(b, 0), 4 * BLOCK, device(a, b_up))
        second_down[r] = send_cand(r, block(b, 0), 4 * BLOCK, device(a, b_down))
        swap[r] = [send_cand(r, block(b, 0), 4 * BLOCK, sibling)]

    def second_pass(r):
        second_up[r].wait_recv()
        pass_up[r] = send_cand(r, block(b_down, 0), 2 * BLOCK, device(a, b_up))
        swap[r].append(send_cand(r, block(b_down, 0), 4 * BLOCK, sibling))
        second_down[r].wait_recv()
        pass_down[r] = send_cand(r, block(b_up, 2), 2 * BLOCK, device(a, b_down))
        swap[r].append(send_cand(r, block(b_up, 0), 4 * BLOCK, sibling))

    def second_end(r):
        pass_up[r].wait_recv()
        swap[r].append(send_cand(r, block(b_far, 0), 2 * BLOCK, sibling))
        pass_down[r].wait_recv()
        swap[r].append(send_cand(r, block(b_far, 2), 2 * BLOCK, sibling))

    def tabulate(r):
        for k in range(ITEMS):
            core_, b_, a_ = k // 16, (k // 4) % 4, k % 4
            ordered[k] = count_ref[r, a_ * (2 + 6 * core_) + b_ * (8 - 6 * core_) + core_]
        ordered[ITEMS] = jnp.int32(0)

        def entry(p, carry):
            k, o, rest = carry
            table[r, p] = jnp.minimum(k, ITEMS - 1) * BLOCK + o
            table[ROUNDS + r, p] = rest
            later = jnp.minimum(k + 1, ITEMS)
            later_count = ordered[later]
            more = rest > 8
            return jnp.where(more, k, later), jnp.where(more, o + 1, 0), jnp.where(more, rest - 8, later_count)

        lax.fori_loop(0, TILES, entry, (jnp.int32(0), jnp.int32(0), ordered[0]), unroll=4)

    def convert(r):
        for copy in swap[r]:
            copy.wait_recv()

        def one(g, carry):
            at = pl.ds(pl.multiple_of(g * (GROUP * 8), GROUP * 8), GROUP * 8)
            place = [table[r, g * GROUP + k] for k in range(GROUP)]
            total = jnp.zeros((GROUP * 8, LANES), F32)
            for q in range(4):
                value = jnp.concatenate(
                    [cand[r][p + q * TILES_SLOTS] for p in place], axis=0
                )
                total += value * value
                value = -2.0 * value
                high = value.astype(BF16)
                ch[r, at, q * LANES:(q + 1) * LANES] = high
                cl[r, at, q * LANES:(q + 1) * LANES] = (value - high.astype(F32)).astype(BF16)
            norm = jnp.broadcast_to(jnp.sum(total, axis=1, keepdims=True), (GROUP * 8, LANES))
            slot = lax.broadcasted_iota(jnp.int32, (8, LANES), 0)
            used = jnp.concatenate(
                [slot < table[ROUNDS + r, g * GROUP + k] for k in range(GROUP)], axis=0
            )
            nrm[r, at, :] = jnp.where(used, norm, jnp.inf)
            return carry

        lax.fori_loop(0, TILES // GROUP, one, 0, unroll=True)

    def prepare(t):
        for copy in near[t] + passed[t]:
            copy.wait_recv()
        total = jnp.zeros((LANES, STEP), F32)
        for q in range(4):
            value = xfull[q, t * STEP:(t + 1) * STEP, :].T
            total += value * value
            high = value.astype(BF16)
            xh[t, q * LANES:(q + 1) * LANES, :] = high
            xl[t, q * LANES:(q + 1) * LANES, :] = (value - high.astype(F32)).astype(BF16)
        sq[t] = jnp.sum(total.reshape(LANES // 8, 8, STEP), axis=0)

    def nearest(t, r):
        high, rows = ch[r], xh[t]
        value = jnp.dot(
            jnp.concatenate([high, cl[r], high], axis=1),
            jnp.concatenate([rows, rows, xl[t]], axis=0),
            preferred_element_type=F32,
        )
        value = value + jnp.concatenate([nrm[r]] * (STEP // LANES), axis=1)
        low[t, r] = jnp.min(value.reshape(TILES, 8, STEP), axis=0)

    def finish(t):
        norm = jnp.sum(sq[t], axis=0, keepdims=True)
        best = [jnp.min(low[t, r], axis=0, keepdims=True) for r in range(ROUNDS)]
        for r in range(1, ROUNDS):
            best[r] = jnp.minimum(best[r], best[r - 1])
        done[:, t * STEP:(t + 1) * STEP] = jnp.concatenate(
            [jnp.maximum(value + norm, 0.0) for value in best], axis=0
        )

    def many(count, body):
        def one(k, carry):
            body(k)
            return carry

        lax.fori_loop(0, count, one, 0)

    pick_send(0)
    count_load.wait()
    tabulate(0)
    pick_send(1)
    first_send(0)
    pick_send(2)
    tabulate(1)
    far_send(0)
    first_send(1)
    far_send(1)
    first_pass(0)
    first_send(2)
    first_pass(1)
    second_send(0)
    near_send(0)
    second_send(1)
    tabulate(2)
    far_send(2)
    far_pass(0)
    second_pass(0)
    near_send(1)
    first_pass(2)
    far_pass(1)
    second_pass(1)
    own_rows.wait()
    prepare(0)
    second_end(0)
    far_pass(2)
    near_send(2)
    second_send(2)
    far_send(3)
    second_end(1)
    convert(0)
    nearest(0, 0)
    convert(1)
    second_pass(2)
    prepare(1)
    near_send(3)
    nearest(1, 0)
    many(2, lambda t: nearest(t, 1))
    second_end(2)
    prepare(2)
    far_pass(3)
    many(2, lambda r: nearest(2, r))
    convert(2)
    many(3, lambda t: nearest(t, 2))
    for t in range(PIECES - 1):
        finish(t)
    for copy in started:
        copy.wait_send()
    started.clear()
    prepare(PIECES - 1)
    many(ROUNDS, lambda r: nearest(PIECES - 1, r))
    finish(PIECES - 1)

    sums = sum([done[:, k * LANES:(k + 1) * LANES] for k in range(SHARE // LANES)])
    line = jnp.concatenate([sums, jnp.zeros((8 - ROUNDS, LANES), F32)], axis=0)
    part[0] = line
    copies = [send(part.at[0], red_line.at[step - 1], line_device(step)) for step in range(1, 8)]
    for step, copy in enumerate(copies):
        copy.wait_recv()
        line = line + red_line[step]
    part[1] = line
    copies = [send(part.at[1], red_plane.at[step - 1], plane_device(step)) for step in range(1, 16)]
    for step, copy in enumerate(copies):
        copy.wait_recv()
        line = line + red_plane[step]
    cost = jnp.sum(line, axis=1, keepdims=True)[:ROUNDS]
    out_ref[...] = jnp.minimum(CAP, TOTAL * done[...] / cost)

    for copy in started:
        copy.wait_send()


COPIES = ROUNDS * 16 + PIECES * 6 + 22
ANY = pl.BlockSpec(memory_space=pl.ANY)


def local(embeddings, cand_index, cand_count):
    return pl.pallas_call(
        kernel,
        out_shape=jax.ShapeDtypeStruct((ROUNDS, SHARE), F32),
        in_specs=[ANY, ANY, ANY],
        out_specs=pl.BlockSpec(memory_space=pltpu.VMEM),
        scratch_shapes=[
            pltpu.SMEM((ROUNDS, SLOTS), jnp.int32),
            pltpu.SMEM((ROUNDS, ITEMS), jnp.int32),
            pltpu.SMEM((ITEMS + 1,), jnp.int32),
            pltpu.SMEM((2 * ROUNDS, TILES), jnp.int32),
            pltpu.VMEM((ROWS, LANES), F32),
            pltpu.VMEM((4, SHARE, LANES), F32),
            pltpu.VMEM((2, PIECES, STEP // 2, LANES), F32),
            *[pltpu.VMEM((ITEMS * BLOCK, TILE, LANES), F32)] * ROUNDS,
            pltpu.VMEM((ROUNDS, USED, 512), BF16),
            pltpu.VMEM((ROUNDS, USED, 512), BF16),
            pltpu.VMEM((ROUNDS, USED, LANES), F32),
            pltpu.VMEM((PIECES, 512, STEP), BF16),
            pltpu.VMEM((PIECES, 512, STEP), BF16),
            pltpu.VMEM((PIECES, 8, STEP), F32),
            pltpu.VMEM((PIECES, ROUNDS, 8, STEP), F32),
            pltpu.VMEM((ROUNDS, SHARE), F32),
            pltpu.VMEM((2, 8, LANES), F32),
            pltpu.VMEM((7, 8, LANES), F32),
            pltpu.VMEM((15, 8, LANES), F32),
            pltpu.SemaphoreType.DMA((4,)),
            pltpu.SemaphoreType.DMA((COPIES,)),
            pltpu.SemaphoreType.DMA((COPIES,)),
        ],
        compiler_params=pltpu.CompilerParams(
            collective_id=0, has_side_effects=True, vmem_limit_bytes=56 * 1024 * 1024
        ),
    )(cand_index, cand_count, embeddings)


def solution(mesh):
    in_specs = (P("item", "dim"), P(None, "item"), P())
    out_specs = P(None, ("item", "dim"))
    return jax.shard_map(local, mesh=mesh, in_specs=in_specs, out_specs=out_specs, check_vma=False)
```

profile of v0, /device:TPU:1, one launch (start us, length us, event | category | flops | bytes accessed | tf_op | source)
XLA Modules:
  0.0 58.6 jit_solution(16022996334489423138)
XLA Ops:
  0.0 57.3 %shard_map.37 = f32[3,1024]{1,0:T(4,128)} custom-call(s32[3,32]{1,0:T(4,128)} %index_hbm.1, s32[3,32]{1,0:T(4,128)} %count_hbm.1, f32[4096,128]{1,0:T(8,128)} %x_ref.1), custom_call_target="tpu_custom_call" | custom-call | tf_op jit(solution)/shard_map/pallas_call | solution.py:330
  57.3 1.3 %copy.5 = f32[3,1024]{1,0:T(4,128)} copy(f32[3,1024]{1,0:T(4,128)} %shard_map.37) | data formatting | bytes 24576
where the time goes:
time: 58.8 us; the launch traced here: 58.6 us
  Pallas kernels  57.3 us (97%)
  local copies, waits for them, and re-layouts  1.33 us (2%)
    pallas_call x1, Pallas kernels, local(): pl.pallas_call(kernel, out_shape=jax.ShapeDtypeStruct((ROUNDS, SHARE), F3...  57.3 us
    unnamed x1, local copies, waits for them, and re-layouts  1.33 us

commit v1 on v0

v1 whole, which is shorter than its diff:
```python
import itertools

import jax
import jax.numpy as jnp
from jax import lax
from jax.experimental import pallas as pl
from jax.experimental.pallas import tpu as pltpu
from jax.sharding import PartitionSpec as P

CAP = 4.0
MESH = pl.DeviceIdType.MESH
ROUNDS = 3
SLOTS = 32
LANES = 128
ITEMS = 32
ROWS = 4096
SHARE = 1024
STEP = 256
PIECES = SHARE // STEP
WIDE = 512
PAIRS = SHARE // WIDE
TOTAL = 131072
TILE = 8
QUARTER = SLOTS // TILE
BLOCK = 4 * QUARTER
BUNDLE = 4 * BLOCK
HALF = 4 * BUNDLE
OFFSET = (0, 3, 1, 2)
TILES = 92
USED = TILES * 8
GROUP = 4
BF16 = jnp.bfloat16
F32 = jnp.float32


def kernel(
    index_hbm, count_hbm, x_ref, out_ref,
    index_ref, count_ref, ordered, table, xv, xfull, relay_buf, cand_0, cand_1, cand_2,
    ch, cl, nrm, xh, xl, sq, low, done, part, red_line, red_plane,
    load_sem, send_sem, recv_sem, cost_sem,
):
    cand = (cand_0, cand_1, cand_2)
    item, dim = lax.axis_index("item"), lax.axis_index("dim")
    z = lax.div(item, 8)
    x = lax.div(item - z * 8, 2)
    core = item - z * 8 - x * 2

    def ring(place):
        return [place] + [jnp.where(place + k > 3, place + k - 4, place + k) for k in range(1, 4)]

    xs, ys, zs = ring(x), ring(dim), ring(z)
    sibling = item + 1 - 2 * core

    def plane(dz, dx):
        return (zs[dz] * 8 + xs[dx] * 2 + core, dim)

    def axis(k, first):
        over_x, over_z = plane(0, k)[0], plane(k, 0)[0]
        lead = 1 - core if first else core
        return (over_z + lead * (over_x - over_z), dim)

    up_a, far_a, down_a = [axis(k, True) for k in range(1, 4)]
    up_b, far_b, down_b = [axis(k, False) for k in range(1, 4)]
    up_y, far_y, down_y = [(item, ys[k]) for k in range(1, 4)]
    _, y_up, y_far, y_down = ys
    line_devices = [(sibling, dim)]
    for k in range(1, 4):
        line_devices += [(item, ys[k]), (sibling, ys[k])]
    plane_devices = [plane(dz, dx) for dz in range(4) for dx in range(4) if dz or dx]

    loads = [
        pltpu.make_async_copy(index_hbm, index_ref, load_sem.at[0]),
        pltpu.make_async_copy(x_ref, xv, load_sem.at[1]),
        pltpu.make_async_copy(count_hbm, count_ref, load_sem.at[2]),
        pltpu.make_async_copy(x_ref.at[pl.ds(dim * SHARE, SHARE)], xfull.at[dim], load_sem.at[3]),
    ]
    for copy in loads:
        copy.start()
    index_load, x_load, count_load, own_rows = loads

    barrier = pltpu.get_barrier_semaphore()
    for target in line_devices + plane_devices:
        pl.semaphore_signal(barrier, inc=1, device_id=target, device_id_type=MESH)

    index_load.wait()
    x_load.wait()
    for r in range(ROUNDS):
        def pick(g, carry, r=r):
            rows = [xv[pl.ds(index_ref[r, g * TILE + k], 1), :] for k in range(TILE)]
            cand[r][core * HALF + dim * QUARTER + g] = jnp.concatenate(rows, axis=0)
            return carry

        lax.fori_loop(0, QUARTER, pick, 0, unroll=True)
    pl.semaphore_wait(barrier, REDUCES)

    number = itertools.count()

    def send(src, dst, target, group):
        k = next(number)
        copy = pltpu.make_async_remote_copy(
            src_ref=src, dst_ref=dst, send_sem=send_sem.at[group], recv_sem=recv_sem.at[k],
            device_id=target, device_id_type=MESH,
        )
        copy.start()
        return copy

    def sent(ref, group):
        pltpu.make_async_copy(ref, ref, send_sem.at[group]).wait()

    half = STEP // 2
    y_copies, first, second, passes, swap, relay, near, passed = [{} for _ in range(8)]

    def near_send(t):
        lands = xfull.at[dim, pl.ds(t * STEP, STEP)]
        near[t] = (
            send(xv.at[pl.ds(y_up * SHARE + t * STEP, STEP)], lands, up_y, NEAR),
            send(xv.at[pl.ds(y_down * SHARE + t * STEP, STEP)], lands, down_y, NEAR),
        )

    def far_send(t):
        far = y_far * SHARE + t * STEP
        relay[t] = (
            send(xv.at[pl.ds(far, half)], relay_buf.at[0, t], up_y, RELAY),
            send(xv.at[pl.ds(far + half, half)], relay_buf.at[1, t], down_y, RELAY),
        )

    def far_pass(t):
        relay[t][0].wait_recv()
        up = send(relay_buf.at[0, t], xfull.at[y_down, pl.ds(t * STEP, half)], up_y, PASSED)
        relay[t][1].wait_recv()
        down = send(relay_buf.at[1, t], xfull.at[y_up, pl.ds(t * STEP + half, half)], down_y, PASSED)
        passed[t] = (up, down)

    def tiles(r, start, count):
        return cand[r].at[pl.ds(core * HALF + start, count)]

    def pick_send(r):
        ref = tiles(r, dim * QUARTER, QUARTER)
        y_copies[r] = [send(ref, ref, target, PICK + r) for target in (up_y, down_y, far_y)]

    def first_send(r):
        for copy in y_copies[r]:
            copy.wait_recv()
        block = tiles(r, 0, BLOCK)
        first[r] = [
            send(block, tiles(r, k * BLOCK, BLOCK), target, FIRST + r)
            for k, target in ((3, far_a), (1, up_a), (2, down_a))
        ]

    def second_send(r):
        for copy in first[r]:
            copy.wait_recv()
        bundle = tiles(r, 0, BUNDLE)
        second[r] = (
            send(bundle, tiles(r, BUNDLE, BUNDLE), up_b, SECOND + r),
            send(bundle, tiles(r, 2 * BUNDLE, BUNDLE), down_b, SECOND + r),
        )
        swap[r] = [send(bundle, bundle, (sibling, dim), SWAP + r)]

    def second_pass(r):
        part = 2 * BLOCK
        second[r][0].wait_recv()
        up = send(tiles(r, BUNDLE, part), tiles(r, 3 * BUNDLE, part), up_b, SECOND + r)
        second[r][1].wait_recv()
        down = send(tiles(r, 2 * BUNDLE + part, part), tiles(r, 3 * BUNDLE + part, part), down_b, SECOND + r)
        passes[r] = (up, down)
        ready = tiles(r, BUNDLE, 2 * BUNDLE)
        swap[r].append(send(ready, ready, (sibling, dim), SWAP + r))

    def second_end(r):
        for copy in passes[r]:
            copy.wait_recv()
        ready = tiles(r, 3 * BUNDLE, BUNDLE)
        swap[r].append(send(ready, ready, (sibling, dim), SWAP + r))

    def tabulate(r):
        for k in range(ITEMS):
            core_, b_, a_ = k // 16, (k // 4) % 4, k % 4
            x_, z_ = xs[OFFSET[b_ if core_ else a_]], zs[OFFSET[a_ if core_ else b_]]
            ordered[k] = count_ref[r, z_ * 8 + x_ * 2 + core_]
        ordered[ITEMS] = jnp.int32(0)

        def entry(p, carry):
            k, o, rest = carry
            table[r, p] = jnp.minimum(k, ITEMS - 1) * BLOCK + o
            table[ROUNDS + r, p] = rest
            later = jnp.minimum(k + 1, ITEMS)
            later_count = ordered[later]
            more = rest > 8
            return jnp.where(more, k, later), jnp.where(more, o + 1, 0), jnp.where(more, rest - 8, later_count)

        lax.fori_loop(0, TILES, entry, (jnp.int32(0), jnp.int32(0), ordered[0]), unroll=4)

    def convert(r):
        for copy in swap[r]:
            copy.wait_recv()

        def one(g, carry):
            at = pl.ds(pl.multiple_of(g * (GROUP * 8), GROUP * 8), GROUP * 8)
            place = [table[r, g * GROUP + k] for k in range(GROUP)]
            total = jnp.zeros((GROUP * 8, LANES), F32)
            for q in range(4):
                value = jnp.concatenate(
                    [cand[r][p + q * QUARTER] for p in place], axis=0
                )
                total += value * value
                value = -2.0 * value
                high = value.astype(BF16)
                ch[r, at, q * LANES:(q + 1) * LANES] = high
                cl[r, at, q * LANES:(q + 1) * LANES] = (value - high.astype(F32)).astype(BF16)
            norm = jnp.broadcast_to(jnp.sum(total, axis=1, keepdims=True), (GROUP * 8, LANES))
            slot = lax.broadcasted_iota(jnp.int32, (8, LANES), 0)
            used = jnp.concatenate(
                [slot < table[ROUNDS + r, g * GROUP + k] for k in range(GROUP)], axis=0
            )
            nrm[r, at, :] = jnp.where(used, norm, jnp.inf)
            return carry

        lax.fori_loop(0, TILES // GROUP, one, 0, unroll=True)

    def prepare(t):
        for copy in near[t] + passed[t]:
            copy.wait_recv()
        at = slice(t % 2 * STEP, (t % 2 + 1) * STEP)
        total = jnp.zeros((LANES, STEP), F32)
        for q in range(4):
            value = xfull[q, t * STEP:(t + 1) * STEP, :].T
            total += value * value
            high = value.astype(BF16)
            xh[t // 2, q * LANES:(q + 1) * LANES, at] = high
            xl[t // 2, q * LANES:(q + 1) * LANES, at] = (value - high.astype(F32)).astype(BF16)
        sq[t // 2, :, at] = jnp.sum(total.reshape(LANES // 8, 8, STEP), axis=0)

    def nearest(t, r):
        high, rows = ch[r], xh[t]
        value = jnp.dot(
            jnp.concatenate([high, cl[r], high], axis=1),
            jnp.concatenate([rows, rows, xl[t]], axis=0),
            preferred_element_type=F32,
        )
        value = value + jnp.concatenate([nrm[r]] * (WIDE // LANES), axis=1)
        low[t, r] = jnp.min(value.reshape(TILES, 8, WIDE), axis=0)

    def finish(t):
        norm = jnp.sum(sq[t], axis=0, keepdims=True)
        best = [jnp.min(low[t, r], axis=0, keepdims=True) for r in range(ROUNDS)]
        for r in range(1, ROUNDS):
            best[r] = jnp.minimum(best[r], best[r - 1])
        done[:, t * WIDE:(t + 1) * WIDE] = jnp.concatenate(
            [jnp.maximum(value + norm, 0.0) for value in best], axis=0
        )

    def many(count, body):
        def one(k, carry):
            body(k)
            return carry

        lax.fori_loop(0, count, one, 0)

    pick_send(0)
    count_load.wait()
    tabulate(0)
    pick_send(1)
    far_send(0)
    first_send(0)
    far_send(1)
    first_send(1)
    near_send(0)
    far_send(2)
    second_send(0)
    far_pass(0)
    tabulate(1)
    pick_send(2)
    second_send(1)
    tabulate(2)
    far_pass(1)
    second_pass(0)
    near_send(1)
    first_send(2)
    own_rows.wait()
    prepare(0)
    second_pass(1)
    near_send(2)
    far_send(3)
    second_end(0)
    far_pass(2)
    second_send(2)
    prepare(1)
    second_end(1)
    near_send(3)
    convert(0)
    nearest(0, 0)
    far_pass(3)
    second_pass(2)
    convert(1)
    nearest(0, 1)
    prepare(2)
    second_end(2)
    prepare(3)
    many(2, lambda r: nearest(1, r))
    for r in range(ROUNDS):
        sent(cand[r].at[pl.ds(0, 3 * QUARTER)], PICK + r)
        sent(cand[r].at[pl.ds(0, 3 * BLOCK)], FIRST + r)
        sent(cand[r].at[pl.ds(0, 3 * BUNDLE)], SECOND + r)
        sent(cand[r].at[pl.ds(0, HALF)], SWAP + r)
    sent(xfull.at[pl.ds(0, 1)], RELAY)
    sent(xfull.at[pl.ds(0, 2)], NEAR)
    sent(xfull.at[pl.ds(0, 1)], PASSED)
    convert(2)
    many(PAIRS, lambda t: nearest(t, 2))
    for t in range(PAIRS):
        finish(t)

    sums = sum([done[:, k * LANES:(k + 1) * LANES] for k in range(SHARE // LANES)])
    line = jnp.concatenate([sums, jnp.zeros((8 - ROUNDS, LANES), F32)], axis=0)
    for stage, (targets, landed) in enumerate(((line_devices, red_line), (plane_devices, red_plane))):
        part[stage] = line
        for k, target in enumerate(targets):
            pltpu.make_async_remote_copy(
                src_ref=part.at[stage], dst_ref=landed.at[k], send_sem=send_sem.at[COST + stage],
                recv_sem=cost_sem.at[stage], device_id=target, device_id_type=MESH,
            ).start()
        pltpu.make_async_copy(landed, landed, cost_sem.at[stage]).wait()
        line = line + jnp.sum(landed[...], axis=0)
    cost = jnp.sum(line, axis=1, keepdims=True)[:ROUNDS]
    out_ref[...] = jnp.minimum(CAP, TOTAL * done[...] / cost)
    sent(red_line, COST)
    sent(red_plane, COST + 1)


COPIES = ROUNDS * 13 + PIECES * 6
REDUCES = 22
PICK, FIRST, SECOND, SWAP, RELAY, NEAR, PASSED, COST = 0, 3, 6, 9, 12, 13, 14, 15
ANY = pl.BlockSpec(memory_space=pl.ANY)


def local(embeddings, cand_index, cand_count):
    return pl.pallas_call(
        kernel,
        out_shape=jax.ShapeDtypeStruct((ROUNDS, SHARE), F32),
        in_specs=[ANY, ANY, ANY],
        out_specs=pl.BlockSpec(memory_space=pltpu.VMEM),
        scratch_shapes=[
            pltpu.SMEM((ROUNDS, SLOTS), jnp.int32),
            pltpu.SMEM((ROUNDS, ITEMS), jnp.int32),
            pltpu.SMEM((ITEMS + 1,), jnp.int32),
            pltpu.SMEM((2 * ROUNDS, TILES), jnp.int32),
            pltpu.VMEM((ROWS, LANES), F32),
            pltpu.VMEM((4, SHARE, LANES), F32),
            pltpu.VMEM((2, PIECES, STEP // 2, LANES), F32),
            *[pltpu.VMEM((ITEMS * BLOCK, TILE, LANES), F32)] * ROUNDS,
            pltpu.VMEM((ROUNDS, USED, 512), BF16),
            pltpu.VMEM((ROUNDS, USED, 512), BF16),
            pltpu.VMEM((ROUNDS, USED, LANES), F32),
            pltpu.VMEM((PAIRS, 512, WIDE), BF16),
            pltpu.VMEM((PAIRS, 512, WIDE), BF16),
            pltpu.VMEM((PAIRS, 8, WIDE), F32),
            pltpu.VMEM((PAIRS, ROUNDS, 8, WIDE), F32),
            pltpu.VMEM((ROUNDS, SHARE), F32),
            pltpu.VMEM((2, 8, LANES), F32),
            pltpu.VMEM((7, 8, LANES), F32),
            pltpu.VMEM((15, 8, LANES), F32),
            pltpu.SemaphoreType.DMA((4,)),
            pltpu.SemaphoreType.DMA((COST + 2,)),
            pltpu.SemaphoreType.DMA((COPIES,)),
            pltpu.SemaphoreType.DMA((2,)),
        ],
        compiler_params=pltpu.CompilerParams(
            collective_id=0, has_side_effects=True, vmem_limit_bytes=56 * 1024 * 1024
        ),
    )(cand_index, cand_count, embeddings)


def solution(mesh):
    in_specs = (P("item", "dim"), P(None, "item"), P())
    out_specs = P(None, ("item", "dim"))
    return jax.shard_map(local, mesh=mesh, in_specs=in_specs, out_specs=out_specs, check_vma=False)
```

time: 58.8 us -> 55.8 us (0.949)
  Pallas kernels: 57.3 us -> 54.3 us
    pallas_call x1, Pallas kernels: 57.3 us -> 54.3 us  [local(): pl.pallas_call(kernel, out_shape=jax.ShapeDtypeStruct((ROUNDS, SHARE), F3...]
where the time goes in v1:
time: 55.8 us; the launch traced here: 55.6 us
  Pallas kernels  54.3 us (97%)
  local copies, waits for them, and re-layouts  1.33 us (2%)
    pallas_call x1, Pallas kernels, local(): pl.pallas_call(kernel, out_shape=jax.ShapeDtypeStruct((ROUNDS, SHARE), F3...  54.3 us
    unnamed x1, local copies, waits for them, and re-layouts  1.33 us

profile of v1, /device:TPU:1, one launch (start us, length us, event | category | flops | bytes accessed | tf_op | source)
XLA Modules:
  0.0 55.6 jit_solution(3800069643301954128)
XLA Ops:
  0.0 54.3 %shard_map.37 = f32[3,1024]{1,0:T(4,128)} custom-call(s32[3,32]{1,0:T(4,128)} %index_hbm.1, s32[3,32]{1,0:T(4,128)} %count_hbm.1, f32[4096,128]{1,0:T(8,128)} %x_ref.1), custom_call_target="tpu_custom_call" | custom-call | tf_op jit(solution)/shard_map/pallas_call | solution.py:338
  54.3 1.3 %copy.5 = f32[3,1024]{1,0:T(4,128)} copy(f32[3,1024]{1,0:T(4,128)} %shard_map.37) | data formatting | bytes 24576
